TPU v7x, 32 devices: a whole 2x2x4 slice. The times are simulated.
32 devices in a mesh: section: 4 (over z), ctx: 8 (over y, x, core).
Axes of the slice: x: 2, y: 2, z: 4, core: 2. Of those that a mesh axis runs over, the one named last changes fastest.
Arguments:
- query_rows: bfloat16 [4, 2048, 2048], P('section', 'ctx'), may hold values from -40 to 40
- key_rows: bfloat16 [4, 2048, 1024], P('section', 'ctx'), may hold values from -6 to 6
- value_rows: bfloat16 [4, 2048, 1024], P('section', 'ctx'), may hold values from -6 to 6
- finished_grad: bfloat16 [4, 2048, 2048], P('section', 'ctx'), may hold values from -96 to 96
- doc_lengths: int32 [4], replicated, may hold values from 1 to 1024, as said below
Outputs:
- query_grad: bfloat16 [4, 2048, 2048], P('section', 'ctx')
- key_grad: bfloat16 [4, 2048, 1024], P('section', 'ctx')
- value_grad: bfloat16 [4, 2048, 1024], P('section', 'ctx')
Inputs may be any that keep to these rules, and one draw needn't show every extreme that they name: `doc_lengths`: document lengths add up to 2048; the longest is exactly 1024.
All inputs are finite; a program needn't handle non-finite values.
Results may differ from a plain program's by a relative error of at most 0.04.
Values may be sent and summed in bfloat16 or wider, within the bound.
A program may use at most 128 MiB of HBM per device.

v0:
```python
import jax
import jax.numpy as jnp
from jax import lax
from jax.sharding import PartitionSpec as P

WINDOW = 1024
KV_HEADS = 8


SCORE_SCALE = 168.0 ** (-0.5)


def passed_along(shard, axis, by):
    count = lax.axis_size(axis)
    return lax.ppermute(shard, axis, [(i, (i + by) % count) for i in range(count)])


def shifted(value, axis, steps):
    count = lax.axis_size(axis)
    initial, last = (max(0, -steps), min(count, count - steps))
    return lax.ppermute(value, axis, [(source, source + steps) for source in range(initial, last)])


def doc_number(positions, doc_lengths):
    ends = jnp.cumsum(doc_lengths)
    return jnp.sum((positions[:, None] >= ends[None, :]).astype(jnp.int32), axis=1)


def window_mask(query_pos, key_pos, doc_lengths):
    same_doc = (
        doc_number(query_pos, doc_lengths)[:, None] == doc_number(key_pos, doc_lengths)[None, :]
    )
    spacing = query_pos[:, None] - key_pos[None, :]
    return same_doc & (spacing >= 0) & (spacing < WINDOW) & (key_pos[None, :] >= 0)


def group_pass(query_part, key_part, value_part, grad_part, allowed):
    count_rows = query_part.shape[0]
    head_size = key_part.shape[1]
    query_head = query_part.reshape(count_rows, -1, head_size)
    grad_head = grad_part.reshape(count_rows, -1, head_size)
    scores = SCORE_SCALE * jnp.einsum(
        "rjd,kd->jrk", query_head, key_part, preferred_element_type=jnp.float32
    )
    scores = jnp.where(allowed[None], scores, -jnp.inf)
    highest = jnp.max(scores, axis=-1, keepdims=True)
    log_total = highest + jnp.log(jnp.sum(jnp.exp(scores - highest), axis=-1, keepdims=True))
    weights = jnp.exp(scores - log_total)
    weight_half = weights.astype(jnp.bfloat16)
    attended = jnp.einsum(
        "jrk,kd->rjd", weight_half, value_part, preferred_element_type=jnp.float32
    ).astype(jnp.bfloat16)
    row_dot = jnp.transpose(
        jnp.sum(attended.astype(jnp.float32) * grad_head.astype(jnp.float32), axis=-1)
    )
    weight_grad = jnp.einsum(
        "rjd,kd->jrk", grad_head, value_part, preferred_element_type=jnp.float32
    )
    score_grad = (weights * (weight_grad - row_dot[:, :, None])).astype(jnp.bfloat16)
    query_back = SCORE_SCALE * jnp.einsum(
        "jrk,kd->rjd", score_grad, key_part, preferred_element_type=jnp.float32
    )
    key_back = SCORE_SCALE * jnp.einsum(
        "jrk,rjd->kd", score_grad, query_head, preferred_element_type=jnp.float32
    )
    value_back = jnp.einsum(
        "jrk,rjd->kd", weight_half, grad_head, preferred_element_type=jnp.float32
    )
    return (query_back.reshape(count_rows, -1), key_back, value_back, log_total[:, :, 0], row_dot)


def local(query_rows, key_rows, value_rows, finished_grad, doc_lengths):
    queries = query_rows[0]
    keys_here = key_rows[0]
    values_here = value_rows[0]
    count_rows = queries.shape[0]
    reach_blocks = WINDOW // count_rows
    pair_width = keys_here.shape[1]
    head_size = pair_width // KV_HEADS
    group_width = queries.shape[1] // KV_HEADS
    heads_group = group_width // head_size
    rank_here = lax.axis_index("ctx")
    first_pos = rank_here * count_rows
    arriving = passed_along(finished_grad, "section", -1)[0]
    own_pair = jnp.stack([keys_here, values_here])
    pieces = [shifted(own_pair, "ctx", distance) for distance in range(reach_blocks, 0, -1)] + [
        own_pair
    ]
    window_pair = jnp.concatenate(pieces, axis=1)
    span = window_pair.shape[1]
    query_pos = first_pos + jnp.arange(count_rows, dtype=jnp.int32)
    key_pos = first_pos - WINDOW + jnp.arange(span, dtype=jnp.int32)
    allowed = window_mask(query_pos, key_pos, doc_lengths)

    def per_group(group, carry):
        query_acc, keys_acc, values_acc, log_totals, row_dots = carry
        query_part = lax.dynamic_slice_in_dim(queries, group * group_width, group_width, 1)
        grad_part = lax.dynamic_slice_in_dim(arriving, group * group_width, group_width, 1)
        key_part = lax.dynamic_slice_in_dim(window_pair[0], group * head_size, head_size, 1)
        value_part = lax.dynamic_slice_in_dim(window_pair[1], group * head_size, head_size, 1)
        query_back, key_back, value_back, log_total, row_dot = group_pass(
            query_part, key_part, value_part, grad_part, allowed
        )
        query_acc = lax.dynamic_update_slice_in_dim(
            query_acc, query_back.astype(jnp.bfloat16), group * group_width, 1
        )
        keys_acc = lax.dynamic_update_slice_in_dim(keys_acc, key_back, group * head_size, 1)
        values_acc = lax.dynamic_update_slice_in_dim(values_acc, value_back, group * head_size, 1)
        log_totals = lax.dynamic_update_slice_in_dim(log_totals, log_total, group * heads_group, 0)
        row_dots = lax.dynamic_update_slice_in_dim(row_dots, row_dot, group * heads_group, 0)
        return (query_acc, keys_acc, values_acc, log_totals, row_dots)

    start_carry = (
        jnp.zeros(queries.shape, jnp.bfloat16),
        jnp.zeros((span, pair_width), jnp.float32),
        jnp.zeros((span, pair_width), jnp.float32),
        jnp.zeros((KV_HEADS * heads_group, count_rows), jnp.float32),
        jnp.zeros((KV_HEADS * heads_group, count_rows), jnp.float32),
    )
    grad_query, grad_keys, grad_values, log_totals, row_dots = lax.fori_loop(
        0, KV_HEADS, per_group, start_carry
    )
    own_start = reach_blocks * count_rows
    grad_pair = jnp.stack([grad_keys, grad_values])
    key_total = grad_pair[:, own_start:]
    for distance in range(1, reach_blocks + 1):
        lower = (reach_blocks - distance) * count_rows
        sent_terms = grad_pair[:, lower : lower + count_rows].astype(jnp.bfloat16)
        key_total = key_total + shifted(sent_terms, "ctx", -distance).astype(jnp.float32)
    return (
        grad_query[None],
        key_total[0].astype(jnp.bfloat16)[None],
        key_total[1].astype(jnp.bfloat16)[None],
    )


def solution(mesh):
    return jax.shard_map(
        local,
        mesh=mesh,
        in_specs=(
            P("section", "ctx", None),
            P("section", "ctx", None),
            P("section", "ctx", None),
            P("section", "ctx", None),
            P(),
        ),
        out_specs=(P("section", "ctx", None), P("section", "ctx", None), P("section", "ctx", None)),
        check_vma=False,
    )
```

profile of v0, /device:TPU:3, one launch (start us, length us, event | category | flops | bytes accessed | tf_op | source)
XLA Modules:
  0.0 287.5 jit_solution(9756623119850137124)
XLA Ops:
  4.5 4.1 %collective-permute-start = (bf16[2,256,1024]{2,1,0:T(8,128)(2,1)}, bf16[2,256,1024]{2,1,0:T(8,128)(2,1)}, u32[]{:S(2)}, u32[]{:S(2)}) collective-permute-start(bf16[2,256,1024]{2,1,0:T(8,128)(2,1)} %constant_dynamic-update-slice_fusion.1), channel_id=1, source_target_pairs={{0,4},{1,5},{2,6},{3,7},{8,12},{9,13},{10,14},{11,15},{16,20},{17,... | collective-permute-start | bytes 3145736 | tf_op jit(solution)/shard_map/ppermute | solution.py:21
  15.0 3.4 %collective-permute-start.4 = (bf16[1,256,2048]{1,2,0:T(8,128)(2,1)S(1)}, bf16[1,256,2048]{1,2,0:T(8,128)(2,1)}, u32[]{:S(2)}, u32[]{:S(2)}) collective-permute-start(bf16[1,256,2048]{1,2,0:T(8,128)(2,1)S(1)} %copy.34), channel_id=1, source_target_pairs={{0,24},{8,0},{16,8},{24,16},{1,25},{9,1},{17,9},{25,17},{2,26},{10... | collective-permute-start | bytes 3145736 | tf_op jit(solution)/shard_map/ppermute | solution.py:15
  20.1 9.7 %collective-permute-done = bf16[2,256,1024]{2,1,0:T(8,128)(2,1)} collective-permute-done((bf16[2,256,1024]{2,1,0:T(8,128)(2,1)}, bf16[2,256,1024]{2,1,0:T(8,128)(2,1)}, u32[]{:S(2)}, u32[]{:S(2)}) %collective-permute-start) | collective-permute-done | bytes 1048608 | tf_op jit(solution)/shard_map/ppermute | solution.py:21
  32.1 10.1 %collective-permute-done.1 = bf16[2,256,1024]{2,1,0:T(8,128)(2,1)} collective-permute-done((bf16[2,256,1024]{2,1,0:T(8,128)(2,1)}, bf16[2,256,1024]{2,1,0:T(8,128)(2,1)}, u32[]{:S(2)}, u32[]{:S(2)}) %collective-permute-start.1) | collective-permute-done | bytes 1048608 | tf_op jit(solution)/shard_map/ppermute | solution.py:21
  44.5 2.3 constant_dynamic-update-slice_fusion.6
  46.8 10.1 %collective-permute-done.3 = bf16[2,256,1024]{2,1,0:T(8,128)(2,1)} collective-permute-done((bf16[2,256,1024]{2,1,0:T(8,128)(2,1)}, bf16[2,256,1024]{2,1,0:T(8,128)(2,1)}, u32[]{:S(2)}, u32[]{:S(2)}) %collective-permute-start.3) | collective-permute-done | bytes 1048608 | tf_op jit(solution)/shard_map/ppermute | solution.py:21
  61.9 3.0 %broadcast.53.clone = f32[1280,1024]{1,0:T(8,128)} broadcast(f32[]{:T(128)} %constant.84.clone.1), dimensions={} | broadcast | bytes 5242884 | tf_op jit(solution)/shard_map/broadcast.7
  64.9 3.0 %broadcast.53 = f32[1280,1024]{1,0:T(8,128)} broadcast(f32[]{:T(128)} %constant.84.clone.1), dimensions={} | broadcast | bytes 5242884 | tf_op jit(solution)/shard_map/broadcast.7
  67.9 99.1 %while.18 = (s32[]{:T(128)}, bf16[256,2048]{1,0:T(8,128)(2,1)}, f32[1280,1024]{1,0:T(8,128)}, f32[1280,1024]{1,0:T(8,128)}, bf16[2,1280,1024]{2,1,0:T(8,128)(2,1...) while((s32[]{:T(128)}, bf16[256,2048]{1,0:T(8,128)(2,1)}, ...), condition=%wide.region_7.8_spmd.clone, body=%wide.region_3.7_spmd.clone.sunk | while | flops 1018067968 | bytes 43159136 | solution.py:120
  70.0 3.1 %fusion.80 = (bf16[1,1280,1024]{2,1,0:T(8,128)(2,1)S(1)}, bf16[1,1280,1024]{2,1,0:T(8,128)(2,1)S(1)}) fusion(bf16[2,1280,1024]{2,1,0:T(8,128)(2,1)} %get-tuple-element.339), kind=kLoop, calls=%fused_computation.67.clone.1 | loop fusion | bytes 10485760 | tf_op jit(solution)/shard_map/while/body/eval_jaxpr/slice | solution.py:100
  82.4 3.1 %fusion.80 = (bf16[1,1280,1024]{2,1,0:T(8,128)(2,1)S(1)}, bf16[1,1280,1024]{2,1,0:T(8,128)(2,1)S(1)}) fusion(bf16[2,1280,1024]{2,1,0:T(8,128)(2,1)} %get-tuple-element.339), kind=kLoop, calls=%fused_computation.67.clone.1 | loop fusion | bytes 10485760 | tf_op jit(solution)/shard_map/while/body/eval_jaxpr/slice | solution.py:100
  94.8 3.1 %fusion.80 = (bf16[1,1280,1024]{2,1,0:T(8,128)(2,1)S(1)}, bf16[1,1280,1024]{2,1,0:T(8,128)(2,1)S(1)}) fusion(bf16[2,1280,1024]{2,1,0:T(8,128)(2,1)} %get-tuple-element.339), kind=kLoop, calls=%fused_computation.67.clone.1 | loop fusion | bytes 10485760 | tf_op jit(solution)/shard_map/while/body/eval_jaxpr/slice | solution.py:100
  107.1 3.1 %fusion.80 = (bf16[1,1280,1024]{2,1,0:T(8,128)(2,1)S(1)}, bf16[1,1280,1024]{2,1,0:T(8,128)(2,1)S(1)}) fusion(bf16[2,1280,1024]{2,1,0:T(8,128)(2,1)} %get-tuple-element.339), kind=kLoop, calls=%fused_computation.67.clone.1 | loop fusion | bytes 10485760 | tf_op jit(solution)/shard_map/while/body/eval_jaxpr/slice | solution.py:100
  119.5 3.1 %fusion.80 = (bf16[1,1280,1024]{2,1,0:T(8,128)(2,1)S(1)}, bf16[1,1280,1024]{2,1,0:T(8,128)(2,1)S(1)}) fusion(bf16[2,1280,1024]{2,1,0:T(8,128)(2,1)} %get-tuple-element.339), kind=kLoop, calls=%fused_computation.67.clone.1 | loop fusion | bytes 10485760 | tf_op jit(solution)/shard_map/while/body/eval_jaxpr/slice | solution.py:100
  131.9 3.1 %fusion.80 = (bf16[1,1280,1024]{2,1,0:T(8,128)(2,1)S(1)}, bf16[1,1280,1024]{2,1,0:T(8,128)(2,1)S(1)}) fusion(bf16[2,1280,1024]{2,1,0:T(8,128)(2,1)} %get-tuple-element.339), kind=kLoop, calls=%fused_computation.67.clone.1 | loop fusion | bytes 10485760 | tf_op jit(solution)/shard_map/while/body/eval_jaxpr/slice | solution.py:100
  144.3 3.1 %fusion.80 = (bf16[1,1280,1024]{2,1,0:T(8,128)(2,1)S(1)}, bf16[1,1280,1024]{2,1,0:T(8,128)(2,1)S(1)}) fusion(bf16[2,1280,1024]{2,1,0:T(8,128)(2,1)} %get-tuple-element.339), kind=kLoop, calls=%fused_computation.67.clone.1 | loop fusion | bytes 10485760 | tf_op jit(solution)/shard_map/while/body/eval_jaxpr/slice | solution.py:100
  156.7 3.1 %fusion.80 = (bf16[1,1280,1024]{2,1,0:T(8,128)(2,1)S(1)}, bf16[1,1280,1024]{2,1,0:T(8,128)(2,1)S(1)}) fusion(bf16[2,1280,1024]{2,1,0:T(8,128)(2,1)} %get-tuple-element.339), kind=kLoop, calls=%fused_computation.67.clone.1 | loop fusion | bytes 10485760 | tf_op jit(solution)/shard_map/while/body/eval_jaxpr/slice | solution.py:100
  167.0 7.7 %fusion.33 = bf16[2,1280,1024]{2,1,0:T(8,128)(2,1)} fusion(f32[1,1280,1024]{2,1,0:T(8,128)} %bitcast.104, f32[1,1280,1024]{2,1,0:T(8,128)} %bitcast.108), kind=kLoop, calls=%fused_computation.47 | loop fusion | flops 2621440 | bytes 15728640 | tf_op jit(solution)/shard_map/convert.6
  174.7 2.9 %fusion.42 = (bf16[2,256,1024]{2,1,0:T(8,128)(2,1)S(1)}, bf16[2,256,1024]{2,1,0:T(8,128)(2,1)S(1)}, bf16[2,256,1024]{2,1,0:T(8,128)(2,1)S(1)}, bf16[2,256,1024]{2,1,0:T(8,128)(2,1)S(1)}) fusion(bf16[2,1280,1024]{2,1,0:T(8,128)(2,1)} %fusion.33), kind=kLoop, calls=%fused_computation.69 | loop fusion | bytes 8388608 | tf_op jit(solution)/shard_map/slice | solution.py:128
  177.6 5.4 %collective-permute-start.5 = (bf16[2,256,1024]{2,1,0:T(8,128)(2,1)S(1)}, bf16[2,256,1024]{2,1,0:T(8,128)(2,1)S(1)}, u32[]{:S(2)}, u32[]{:S(2)}) collective-permute-start(bf16[2,256,1024]{2,1,0:T(8,128)(2,1)S(1)} %get-tuple-element.208), channel_id=1, source_target_pairs={{1,0},{2,1},{3,2},{4,3},{5,4},{6,5},{7,6},{9,8},{10,9},{11,10},{12... | collective-permute-start | bytes 3145736 | tf_op jit(solution)/shard_map/ppermute | solution.py:21
  184.3 25.5 %collective-permute-start.7 = (bf16[2,256,1024]{2,1,0:T(8,128)(2,1)S(1)}, bf16[2,256,1024]{2,1,0:T(8,128)(2,1)S(1)}, u32[]{:S(2)}, u32[]{:S(2)}) collective-permute-start(bf16[2,256,1024]{2,1,0:T(8,128)(2,1)S(1)} %get-tuple-element.210), channel_id=1, source_target_pairs={{3,0},{4,1},{5,2},{6,3},{7,4},{11,8},{12,9},{13,10},{14,11},{15,12... | collective-permute-start | bytes 3145736 | tf_op jit(solution)/shard_map/ppermute | solution.py:21
  209.8 9.4 %collective-permute-start.6 = (bf16[2,256,1024]{2,1,0:T(8,128)(2,1)S(1)}, bf16[2,256,1024]{2,1,0:T(8,128)(2,1)S(1)}, u32[]{:S(2)}, u32[]{:S(2)}) collective-permute-start(bf16[2,256,1024]{2,1,0:T(8,128)(2,1)S(1)} %get-tuple-element.211), channel_id=1, source_target_pairs={{2,0},{3,1},{4,2},{5,3},{6,4},{7,5},{10,8},{11,9},{12,10},{13,11},... | collective-permute-start | bytes 3145736 | tf_op jit(solution)/shard_map/ppermute | solution.py:21
  219.1 18.3 %collective-permute-done.5 = bf16[2,256,1024]{2,1,0:T(8,128)(2,1)S(1)} collective-permute-done((bf16[2,256,1024]{2,1,0:T(8,128)(2,1)S(1)}, bf16[2,256,1024]{2,1,0:T(8,128)(2,1)S(1)}, u32[]{:S(2)}, u32[]{:S(2)}) %collective-permute-start.5) | collective-permute-done | bytes 1048608 | tf_op jit(solution)/shard_map/ppermute | solution.py:21
  237.5 48.0 %collective-permute-done.7 = bf16[2,256,1024]{2,1,0:T(8,128)(2,1)S(1)} collective-permute-done((bf16[2,256,1024]{2,1,0:T(8,128)(2,1)S(1)}, bf16[2,256,1024]{2,1,0:T(8,128)(2,1)S(1)}, u32[]{:S(2)}, u32[]{:S(2)}) %collective-permute-start.7) | collective-permute-done | bytes 1048608 | tf_op jit(solution)/shard_map/ppermute | solution.py:21
  (174 shorter events, 98.5 us)
Async XLA Ops:
  0.6 13.8 %copy-start.4 = (bf16[1,256,2048]{2,1,0:T(8,128)(2,1)S(1)}, bf16[1,256,2048]{2,1,0:T(8,128)(2,1)}, u32[]{:S(2)}) copy-start(bf16[1,256,2048]{2,1,0:T(8,128)(2,1)} %param.10) | copy-start | bytes 3145732
  0.6 17.7 %copy-start.6 = (s32[4]{0:T(128)S(1)}, s32[4]{0:T(128)}, u32[]{:S(2)}) copy-start(s32[4]{0:T(128)} %param.11) | copy-start | bytes 52
  0.7 17.9 %copy-start.5 = (bf16[1,256,2048]{2,1,0:T(8,128)(2,1)S(1)}, bf16[1,256,2048]{2,1,0:T(8,128)(2,1)}, u32[]{:S(2)}) copy-start(bf16[1,256,2048]{2,1,0:T(8,128)(2,1)} %param.7) | copy-start | bytes 3145732
  4.5 25.3 %collective-permute-start = (bf16[2,256,1024]{2,1,0:T(8,128)(2,1)}, bf16[2,256,1024]{2,1,0:T(8,128)(2,1)}, u32[]{:S(2)}, u32[]{:S(2)}) collective-permute-start(bf16[2,256,1024]{2,1,0:T(8,128)(2,1)} %constant_dynamic-update-slice_fusion.1), channel_id=1, source_target_pairs={{0,4},{1,5},{2,6},{3,7},{8,12},{9,13},{10,14},{11,15},{16,20},{17,... | collective-permute-start | bytes 3145736 | tf_op jit(solution)/shard_map/ppermute | solution.py:21
  8.7 33.5 %collective-permute-start.1 = (bf16[2,256,1024]{2,1,0:T(8,128)(2,1)}, bf16[2,256,1024]{2,1,0:T(8,128)(2,1)}, u32[]{:S(2)}, u32[]{:S(2)}) collective-permute-start(bf16[2,256,1024]{2,1,0:T(8,128)(2,1)} %constant_dynamic-update-slice_fusion.1), channel_id=1, source_target_pairs={{0,3},{1,4},{2,5},{3,6},{4,7},{8,11},{9,12},{10,13},{11,14},{12,15... | collective-permute-start | bytes 3145736 | tf_op jit(solution)/shard_map/ppermute | solution.py:21
  10.6 33.9 %collective-permute-start.2 = (bf16[2,256,1024]{2,1,0:T(8,128)(2,1)}, bf16[2,256,1024]{2,1,0:T(8,128)(2,1)}, u32[]{:S(2)}, u32[]{:S(2)}) collective-permute-start(bf16[2,256,1024]{2,1,0:T(8,128)(2,1)} %constant_dynamic-update-slice_fusion.1), channel_id=1, source_target_pairs={{0,2},{1,3},{2,4},{3,5},{4,6},{5,7},{8,10},{9,11},{10,12},{11,13},... | collective-permute-start | bytes 3145736 | tf_op jit(solution)/shard_map/ppermute | solution.py:21
  12.5 44.4 %collective-permute-start.3 = (bf16[2,256,1024]{2,1,0:T(8,128)(2,1)}, bf16[2,256,1024]{2,1,0:T(8,128)(2,1)}, u32[]{:S(2)}, u32[]{:S(2)}) collective-permute-start(bf16[2,256,1024]{2,1,0:T(8,128)(2,1)} %constant_dynamic-update-slice_fusion.1), channel_id=1, source_target_pairs={{0,1},{1,2},{2,3},{3,4},{4,5},{5,6},{6,7},{8,9},{9,10},{10,11},{11... | collective-permute-start | bytes 3145736 | tf_op jit(solution)/shard_map/ppermute | solution.py:21
  15.0 45.9 %collective-permute-start.4 = (bf16[1,256,2048]{1,2,0:T(8,128)(2,1)S(1)}, bf16[1,256,2048]{1,2,0:T(8,128)(2,1)}, u32[]{:S(2)}, u32[]{:S(2)}) collective-permute-start(bf16[1,256,2048]{1,2,0:T(8,128)(2,1)S(1)} %copy.34), channel_id=1, source_target_pairs={{0,24},{8,0},{16,8},{24,16},{1,25},{9,1},{17,9},{25,17},{2,26},{10... | collective-permute-start | bytes 3145736 | tf_op jit(solution)/shard_map/ppermute | solution.py:15
  32.1 27.0 %copy-start.2 = (bf16[1,256,1024]{2,1,0:T(8,128)(2,1)S(1)}, bf16[1,256,1024]{2,1,0:T(8,128)(2,1)}, u32[]{:S(2)}) copy-start(bf16[1,256,1024]{2,1,0:T(8,128)(2,1)} %param.8) | copy-start | bytes 1572868
  44.5 15.5 %copy-start.3 = (bf16[1,256,1024]{2,1,0:T(8,128)(2,1)S(1)}, bf16[1,256,1024]{2,1,0:T(8,128)(2,1)}, u32[]{:S(2)}) copy-start(bf16[1,256,1024]{2,1,0:T(8,128)(2,1)} %param.9) | copy-start | bytes 1572868
  76.8 2.1 copy-start.1
  89.2 2.1 copy-start.1
  101.6 2.1 copy-start.1
  126.3 2.1 copy-start.1
  138.7 2.1 copy-start.1
  163.5 2.1 copy-start.1
  167.0 118.5 %slice-start = ((s8[5242880]{0:T(1024)(128)(4,1)}), s8[4194304]{0:T(1024)(128)(4,1)S(1)}, s32[]{:S(2)}) async-start(s8[5242880]{0:T(1024)(128)(4,1)} %bitcast.105), calls=%async_computation | async-start | bytes 8388608
  167.0 118.5 %slice-start.2 = ((s8[5242880]{0:T(1024)(128)(4,1)}), s8[4194304]{0:T(1024)(128)(4,1)S(1)}, s32[]{:S(2)}) async-start(s8[5242880]{0:T(1024)(128)(4,1)} %bitcast.109), calls=%async_computation.2 | async-start | bytes 8388608
  167.0 118.5 %slice-start.1 = ((s8[5242880]{0:T(1024)(128)(4,1)}), s8[1048576]{0:T(1024)(128)(4,1)S(1)}, s32[]{:S(2)}) async-start(s8[5242880]{0:T(1024)(128)(4,1)} %bitcast.105), calls=%async_computation.1 | async-start | bytes 2097152
  167.0 118.5 %slice-start.3 = ((s8[5242880]{0:T(1024)(128)(4,1)}), s8[1048576]{0:T(1024)(128)(4,1)S(1)}, s32[]{:S(2)}) async-start(s8[5242880]{0:T(1024)(128)(4,1)} %bitcast.109), calls=%async_computation.3 | async-start | bytes 2097152
  177.6 59.9 %collective-permute-start.5 = (bf16[2,256,1024]{2,1,0:T(8,128)(2,1)S(1)}, bf16[2,256,1024]{2,1,0:T(8,128)(2,1)S(1)}, u32[]{:S(2)}, u32[]{:S(2)}) collective-permute-start(bf16[2,256,1024]{2,1,0:T(8,128)(2,1)S(1)} %get-tuple-element.208), channel_id=1, source_target_pairs={{1,0},{2,1},{3,2},{4,3},{5,4},{6,5},{7,6},{9,8},{10,9},{11,10},{12... | collective-permute-start | bytes 3145736 | tf_op jit(solution)/shard_map/ppermute | solution.py:21
  183.0 54.5 %collective-permute-start.8 = (bf16[2,256,1024]{2,1,0:T(8,128)(2,1)S(1)}, bf16[2,256,1024]{2,1,0:T(8,128)(2,1)S(1)}, u32[]{:S(2)}, u32[]{:S(2)}) collective-permute-start(bf16[2,256,1024]{2,1,0:T(8,128)(2,1)S(1)} %get-tuple-element.209), channel_id=1, source_target_pairs={{4,0},{5,1},{6,2},{7,3},{12,8},{13,9},{14,10},{15,11},{20,16},{21,... | collective-permute-start | bytes 3145736 | tf_op jit(solution)/shard_map/ppermute | solution.py:21
  184.3 101.2 %collective-permute-start.7 = (bf16[2,256,1024]{2,1,0:T(8,128)(2,1)S(1)}, bf16[2,256,1024]{2,1,0:T(8,128)(2,1)S(1)}, u32[]{:S(2)}, u32[]{:S(2)}) collective-permute-start(bf16[2,256,1024]{2,1,0:T(8,128)(2,1)S(1)} %get-tuple-element.210), channel_id=1, source_target_pairs={{3,0},{4,1},{5,2},{6,3},{7,4},{11,8},{12,9},{13,10},{14,11},{15,12... | collective-permute-start | bytes 3145736 | tf_op jit(solution)/shard_map/ppermute | solution.py:21
  209.8 75.7 %collective-permute-start.6 = (bf16[2,256,1024]{2,1,0:T(8,128)(2,1)S(1)}, bf16[2,256,1024]{2,1,0:T(8,128)(2,1)S(1)}, u32[]{:S(2)}, u32[]{:S(2)}) collective-permute-start(bf16[2,256,1024]{2,1,0:T(8,128)(2,1)S(1)} %get-tuple-element.211), channel_id=1, source_target_pairs={{2,0},{3,1},{4,2},{5,3},{6,4},{7,5},{10,8},{11,9},{12,10},{13,11},... | collective-permute-start | bytes 3145736 | tf_op jit(solution)/shard_map/ppermute | solution.py:21
  (10 other events, 12.7 us)
where the time goes:
time: 288 us
  waiting for transfers between devices  96.2 us (33%)
  local copies, waits for them, and re-layouts  75 us (26%)
  starting transfers between devices  54.8 us (19%)
  matrix products  39.3 us (14%)
  other arithmetic  20.8 us (7%)
    ppermute x8, waiting for transfers between devices, shifted(): lax.ppermute(value, axis, [(source, source + steps) for source in range(i...  96.2 us
    ppermute x8, starting transfers between devices, shifted(): lax.ppermute(value, axis, [(source, source + steps) for source in range(i...  51.4 us
    slice x8, local copies, waits for them, and re-layouts, per_group(): window_pair[1]  24.9 us
    unnamed x26, local copies, waits for them, and re-layouts  13.9 us
    dot_general x8, matrix products, group_pass(): jnp.einsum('jrk,rjd->kd', weight_half, grad_head, preferred_element_type=...  11.4 us
    dot_general x8, matrix products, group_pass(): jnp.einsum('jrk,rjd->kd', score_grad, query_head, preferred_element_type=...  11.1 us
    another operation x3, other arithmetic  8.87 us
    and x8, other arithmetic, window_mask(): same_doc & (spacing >= 0) & (spacing < WINDOW) & (key_pos[None, :] >= 0)  8.76 us
  transfers between devices with their start and end apart: 9, of which 5 were waited for; matrix products, arithmetic and copies ran while one was open for 5% of the time, Pallas kernels for 0%

commit v1 on v0

v1 whole, which is shorter than its diff:
```python
import functools
import math

import jax
import jax.numpy as jnp
from jax import lax
from jax.experimental import pallas as pl
from jax.experimental.pallas import tpu as pltpu
from jax.sharding import PartitionSpec as P

WINDOW = 1024
KV_HEADS = 8
CORES = 2
TILE = 128

SCORE_SCALE = 168.0 ** (-0.5)
SCORE_SCALE_LOG2 = SCORE_SCALE * math.log2(math.e)
MESH = pl.DeviceIdType.MESH


def kernel(
    sections, chips,
    docs, q_in, k_in, v_in, o_in,
    dq_out, dk_out, dv_out,
    q_buf, o_buf, kv_buf, kt_buf, bias_buf, acc_k, acc_v, term_buf, got_buf, dq_buf,
    q_send, q_recv, o_send, o_recv, kv_send, kv_recv, g_send, g_recv, dq_send, dq_recv, dq_local,
):
    local_heads, chip_rows, group_width = q_buf.shape
    head_size = kt_buf.shape[0]
    rows = chip_rows // CORES
    reach = WINDOW // chip_rows
    own_start = reach * chip_rows
    width = WINDOW + TILE
    tiles = chip_rows // TILE
    sec = lax.axis_index("section")
    rank = lax.axis_index("ctx")
    chip = rank // CORES
    core = rank % CORES
    other = 1 - core
    sibling = chip * CORES + other
    sec_from = lax.rem(sec + 1, sections)
    sec_to = lax.rem(sec + sections - 1, sections)

    barrier = pltpu.get_barrier_semaphore()

    def greet(section, ctx):
        pl.semaphore_signal(barrier, inc=1, device_id=(section, ctx), device_id_type=MESH)

    greet(sec, sibling)
    for t in range(CORES):
        greet(sec_from, chip * CORES + t)
        greet(sec_to, chip * CORES + t)
    for away in range(1, reach + 1):
        @pl.when(chip >= away)
        def _():
            for t in range(CORES):
                greet(sec, (chip - away) * CORES + t)

        @pl.when(chip + away < chips)
        def _():
            for t in range(CORES):
                greet(sec, (chip + away) * CORES + t)
    peers = jnp.int32(1 + 2 * CORES)
    for away in range(1, reach + 1):
        peers = peers + jnp.where(chip >= away, CORES, 0) + jnp.where(chip + away < chips, CORES, 0)
    pl.semaphore_wait(barrier, peers)

    def aligned(start, size):
        return pl.ds(pl.multiple_of(start, size), size)

    def rows_of(c):
        return aligned(c * rows, rows)

    def group_cols(h, t):
        return aligned((t * local_heads + h) * group_width, group_width)

    def head_cols(h, t):
        return aligned((t * local_heads + h) * head_size, head_size)

    def copy_o(h, t, from_core):
        return pltpu.make_async_remote_copy(
            src_ref=o_in.at[0, :, group_cols(h, t)],
            dst_ref=o_buf.at[h, rows_of(from_core), :],
            send_sem=o_send.at[h, t],
            recv_sem=o_recv.at[h, from_core],
            device_id=(sec_to, chip * CORES + t),
            device_id_type=MESH,
        )

    def copy_q_sibling(h, from_core):
        return pltpu.make_async_remote_copy(
            src_ref=q_in.at[0, :, group_cols(h, other)],
            dst_ref=q_buf.at[h, rows_of(from_core), :],
            send_sem=q_send.at[h],
            recv_sem=q_recv.at[h, 1],
            device_id=(sec, sibling),
            device_id_type=MESH,
        )

    def copy_q_own(h):
        return pltpu.make_async_copy(
            q_in.at[0, :, group_cols(h, core)], q_buf.at[h, rows_of(core), :], q_recv.at[h, 0]
        )

    def kv_rows(away, c):
        return aligned((reach - away) * chip_rows + c * rows, rows)

    def copy_kv(h, which, away, t, from_core):
        source = (k_in, v_in)[which]
        return pltpu.make_async_remote_copy(
            src_ref=source.at[0, :, head_cols(h, t)],
            dst_ref=kv_buf.at[h, which, kv_rows(away, from_core), :],
            send_sem=kv_send.at[h, which, away * CORES + t],
            recv_sem=kv_recv.at[h, which, away * CORES + from_core],
            device_id=(sec, (chip + away) * CORES + t),
            device_id_type=MESH,
        )

    def copy_kv_own(h, which):
        source = (k_in, v_in)[which]
        return pltpu.make_async_copy(
            source.at[0, :, head_cols(h, core)],
            kv_buf.at[h, which, kv_rows(0, core), :],
            kv_recv.at[h, which, core],
        )

    def copy_term(h, away, t):
        return pltpu.make_async_remote_copy(
            src_ref=term_buf.at[h, :, kv_rows(away, t), :],
            dst_ref=got_buf.at[away, core * local_heads + h],
            send_sem=g_send.at[h, away * CORES + t],
            recv_sem=g_recv.at[away, core * local_heads + h],
            device_id=(sec, (chip - away) * CORES + t),
            device_id_type=MESH,
        )

    def wait_term(g, away):
        pltpu.make_async_remote_copy(
            src_ref=term_buf.at[0, :, pl.ds(0, rows), :],
            dst_ref=got_buf.at[away, g],
            send_sem=g_send.at[0, 0],
            recv_sem=g_recv.at[away, g],
            device_id=(sec, sibling),
            device_id_type=MESH,
        ).wait_recv()

    def copy_term_own(h):
        return pltpu.make_async_copy(
            term_buf.at[h, :, kv_rows(0, core), :],
            got_buf.at[0, core * local_heads + h],
            g_recv.at[0, core * local_heads + h],
        )

    def copy_dq_sibling(h, for_core):
        return pltpu.make_async_remote_copy(
            src_ref=dq_buf.at[h, rows_of(for_core), :],
            dst_ref=dq_out.at[0, :, group_cols(h, 1 - for_core)],
            send_sem=dq_send.at[h],
            recv_sem=dq_recv.at[h],
            device_id=(sec, sibling),
            device_id_type=MESH,
        )

    def copy_dq_own(h):
        return pltpu.make_async_copy(
            dq_buf.at[h, rows_of(core), :], dq_out.at[0, :, group_cols(h, core)], dq_local.at[h]
        )

    @pl.loop(0, local_heads)
    def _(h):
        for t in range(CORES):
            copy_o(h, t, core).start()
        for which in range(2):
            for away in range(1, reach + 1):
                @pl.when(chip + away < chips)
                def _():
                    for t in range(CORES):
                        copy_kv(h, which, away, t, core).start()
        copy_q_sibling(h, core).start()
        copy_q_own(h).start()
        for which in range(2):
            copy_kv(h, which, 0, other, core).start()
            copy_kv_own(h, which).start()

    for away in range(1, reach + 1):
        @pl.when(chip < away)
        def _():
            kv_buf[:, :, pl.ds((reach - away) * chip_rows, chip_rows), :] = jnp.zeros(
                (local_heads, 2, chip_rows, head_size), kv_buf.dtype
            )

        @pl.when(chip + away >= chips)
        def _():
            got_buf[away] = jnp.zeros(got_buf.shape[1:], got_buf.dtype)

    for tile in range(tiles):
        query_pos = chip * chip_rows + tile * TILE + lax.broadcasted_iota(jnp.int32, (1, TILE), 1)
        lowest = query_pos - (WINDOW - 1)
        end = jnp.int32(0)
        lowest = jnp.maximum(lowest, 0)
        for d in range(docs.shape[0]):
            end = end + docs[d]
            lowest = jnp.maximum(lowest, jnp.where(query_pos >= end, end, 0))
        key_pos = (
            chip * chip_rows - WINDOW + tile * TILE
            + lax.broadcasted_iota(jnp.int32, (width, TILE), 0)
        )
        bias_buf[tile] = jnp.where(
            (key_pos <= query_pos) & (key_pos >= lowest), 0.0, -jnp.inf
        ).astype(jnp.float32)

    def two_heads(block):
        return jnp.concatenate([block[:, :head_size], block[:, head_size:]], axis=0)

    @pl.loop(0, local_heads)
    def _(h):
        copy_q_own(h).wait()
        copy_q_sibling(h, other).wait_recv()
        for which in range(2):
            copy_kv_own(h, which).wait()
            copy_kv(h, which, 0, other, other).wait_recv()
        for c in range(CORES):
            copy_o(h, c, c).wait_recv()
        for away in range(1, reach + 1):
            @pl.when(chip >= away)
            def _():
                for which in range(2):
                    for c in range(CORES):
                        copy_kv(h, which, away, c, c).wait_recv()

        kt_buf[...] = kv_buf[h, 0].T
        acc_k[...] = jnp.zeros_like(acc_k)
        acc_v[...] = jnp.zeros_like(acc_v)

        @pl.loop(0, tiles)
        def _(tile):
            span = pl.ds(pl.multiple_of(tile * TILE, TILE), width)
            here = aligned(tile * TILE, TILE)
            keys = kv_buf[h, 0, span, :]
            values = kv_buf[h, 1, span, :]
            queries = two_heads(q_buf[h, here, :])
            grads = two_heads(o_buf[h, here, :])
            bias = bias_buf[tile]
            nt = (((1,), (1,)), ((), ()))
            scores = lax.dot_general(keys, queries, nt, preferred_element_type=jnp.float32)
            scores = scores * SCORE_SCALE_LOG2 + jnp.concatenate([bias, bias], axis=1)
            highest = jnp.max(scores, axis=0, keepdims=True)
            raised = jnp.exp2(scores - highest)
            weights = raised * (1.0 / jnp.sum(raised, axis=0, keepdims=True))
            weight_grad = lax.dot_general(values, grads, nt, preferred_element_type=jnp.float32)
            row_dot = jnp.sum(weights * weight_grad, axis=0, keepdims=True)
            score_grad = (weights * (weight_grad - row_dot)).astype(jnp.bfloat16)
            weight_half = weights.astype(jnp.bfloat16)
            acc_v[span, :] += jnp.dot(weight_half, grads, preferred_element_type=jnp.float32)
            acc_k[span, :] += jnp.dot(score_grad, queries, preferred_element_type=jnp.float32)
            back = jnp.dot(kt_buf[:, span], score_grad, preferred_element_type=jnp.float32)
            back = (back * SCORE_SCALE).T.astype(jnp.bfloat16)
            dq_buf[h, here, :] = jnp.concatenate([back[:TILE], back[TILE:]], axis=1)

        term_buf[h, 0] = (acc_k[...] * SCORE_SCALE).astype(jnp.bfloat16)
        term_buf[h, 1] = acc_v[...].astype(jnp.bfloat16)
        for away in range(1, reach + 1):
            @pl.when(chip >= away)
            def _():
                for t in range(CORES):
                    copy_term(h, away, t).start()
        copy_term(h, 0, other).start()
        copy_term_own(h).start()
        copy_dq_sibling(h, other).start()
        copy_dq_own(h).start()

    @pl.loop(0, local_heads)
    def _(h):
        copy_term_own(h).wait()
        wait_term(other * local_heads + h, 0)
        for away in range(1, reach + 1):
            @pl.when(chip + away < chips)
            def _():
                for t in range(CORES):
                    wait_term(t * local_heads + h, away)
        for t in range(CORES):
            g = t * local_heads + h
            total = got_buf[0, g].astype(jnp.float32)
            for away in range(1, reach + 1):
                total = total + got_buf[away, g].astype(jnp.float32)
            dk_out[0, :, head_cols(h, t)] = total[0].astype(jnp.bfloat16)
            dv_out[0, :, head_cols(h, t)] = total[1].astype(jnp.bfloat16)

    @pl.loop(0, local_heads)
    def _(h):
        copy_dq_own(h).wait()
        copy_dq_sibling(h, core).wait_recv()
        copy_dq_sibling(h, other).wait_send()
        copy_q_sibling(h, core).wait_send()
        for t in range(CORES):
            copy_o(h, t, core).wait_send()
        for which in range(2):
            copy_kv(h, which, 0, other, core).wait_send()
        copy_term(h, 0, other).wait_send()
        for away in range(1, reach + 1):
            @pl.when(chip + away < chips)
            def _():
                for which in range(2):
                    for t in range(CORES):
                        copy_kv(h, which, away, t, core).wait_send()

            @pl.when(chip >= away)
            def _():
                for t in range(CORES):
                    copy_term(h, away, t).wait_send()


def local(sections, chips, query_rows, key_rows, value_rows, finished_grad, doc_lengths):
    rows = query_rows.shape[1]
    kv_width = key_rows.shape[2]
    head_size = kv_width // KV_HEADS
    group_width = query_rows.shape[2] // KV_HEADS
    local_heads = KV_HEADS // CORES
    chip_rows = CORES * rows
    reach = WINDOW // chip_rows
    span = WINDOW + chip_rows
    half = jnp.bfloat16
    dma = pltpu.SemaphoreType.DMA
    anywhere = pl.BlockSpec(memory_space=pl.ANY)
    in_vmem = pl.BlockSpec(memory_space=pltpu.VMEM)
    pairs = 2 * (KV_HEADS // 2) * chip_rows * (WINDOW + TILE)
    return pl.pallas_call(
        functools.partial(kernel, sections, chips),
        out_shape=(
            jax.ShapeDtypeStruct(query_rows.shape, half),
            jax.ShapeDtypeStruct(key_rows.shape, half),
            jax.ShapeDtypeStruct(value_rows.shape, half),
        ),
        in_specs=[pl.BlockSpec(memory_space=pltpu.SMEM)] + [anywhere] * 4,
        out_specs=(anywhere, in_vmem, in_vmem),
        scratch_shapes=[
            pltpu.VMEM((local_heads, chip_rows, group_width), half),
            pltpu.VMEM((local_heads, chip_rows, group_width), half),
            pltpu.VMEM((local_heads, 2, span, head_size), half),
            pltpu.VMEM((head_size, span), half),
            pltpu.VMEM((chip_rows // TILE, WINDOW + TILE, TILE), jnp.float32),
            pltpu.VMEM((span, head_size), jnp.float32),
            pltpu.VMEM((span, head_size), jnp.float32),
            pltpu.VMEM((local_heads, 2, span, head_size), half),
            pltpu.VMEM((reach + 1, KV_HEADS, 2, rows, head_size), half),
            pltpu.VMEM((local_heads, chip_rows, group_width), half),
            dma((local_heads,)),
            dma((local_heads, 2)),
            dma((local_heads, CORES)),
            dma((local_heads, CORES)),
            dma((local_heads, 2, (reach + 1) * CORES)),
            dma((local_heads, 2, (reach + 1) * CORES)),
            dma((local_heads, (reach + 1) * CORES)),
            dma((reach + 1, KV_HEADS)),
            dma((local_heads,)),
            dma((local_heads,)),
            dma((local_heads,)),
        ],
        compiler_params=pltpu.CompilerParams(
            collective_id=0, has_side_effects=True, vmem_limit_bytes=48 * 1024 * 1024
        ),
        cost_estimate=pl.CostEstimate(
            flops=10 * pairs * head_size, bytes_accessed=8 * 1024 * 1024, transcendentals=pairs
        ),
    )(doc_lengths, query_rows, key_rows, value_rows, finished_grad)


def solution(mesh):
    spec = P("section", "ctx", None)
    return jax.shard_map(
        functools.partial(local, mesh.shape["section"], mesh.shape["ctx"] // CORES),
        mesh=mesh,
        in_specs=(spec, spec, spec, spec, P()),
        out_specs=(spec, spec, spec),
        check_vma=False,
    )
```

time: 288 us -> 78.2 us (0.27)
  waiting for transfers between devices: 96.2 us -> 0 us
  Pallas kernels: 0 us -> 68.7 us
  local copies, waits for them, and re-layouts: 75 us -> 7.74 us
  starting transfers between devices: 54.8 us -> 0 us
  matrix products: 39.3 us -> 0 us
  other arithmetic: 20.8 us -> 0 us
    ppermute x9 -> x0, waiting for transfers between devices: 96.2 us -> none  [the longest x8 96.2 us: shifted(): lax.ppermute(value, axis, [(source, source + steps) for source in range(i...]
    pallas_call x0 -> x1, Pallas kernels: none -> 68.7 us  [local(): pl.pallas_call(functools.partial(kernel, sections, chips), out_shape=(jax...]
    ppermute x9 -> x0, starting transfers between devices: 54.8 us -> none  [the longest x8 51.4 us: shifted(): lax.ppermute(value, axis, [(source, source + steps) for source in range(i...]
    dot_general x48 -> x0, matrix products: 39.3 us -> none  [the longest x8 11.4 us: group_pass(): jnp.einsum('jrk,rjd->kd', weight_half, grad_head, preferred_element_type=...]
    slice x10 -> x0, local copies, waits for them, and re-layouts: 28.8 us -> none  [the longest x8 24.9 us: per_group(): window_pair[1]]
    another operation x3 -> x0, other arithmetic: 8.87 us -> none
    and x8 -> x0, other arithmetic: 8.76 us -> none  [window_mask(): same_doc & (spacing >= 0) & (spacing < WINDOW) & (key_pos[None, :] >= 0)]
    while x32 -> x0, local copies, waits for them, and re-layouts: 8.52 us -> none
  transfers between devices with their start and end apart: 9 -> 0, of which waited for: 5 -> 0; matrix products, arithmetic and copies ran while one was open for 5% -> 0% of each run, Pallas kernels for 0% -> 0%
where the time goes in v1:
time: 78.2 us; the launch traced here: 77.1 us
  Pallas kernels  68.7 us (88%)
  local copies, waits for them, and re-layouts  7.74 us (10%)
    pallas_call x1, Pallas kernels, local(): pl.pallas_call(functools.partial(kernel, sections, chips), out_shape=(jax...  68.7 us
    unnamed x13, local copies, waits for them, and re-layouts  7.74 us

profile of v1, /device:TPU:3, one launch (start us, length us, event | category | flops | bytes accessed | tf_op | source)
XLA Modules:
  0.0 77.1 jit_solution(5784117505378300467)
XLA Ops:
  0.6 0.0 copy-start
  0.6 1.2 %copy-done = bf16[1,256,2048]{2,1,0:T(8,128)(2,1)S(1)} copy-done((bf16[1,256,2048]{2,1,0:T(8,128)(2,1)S(1)}, bf16[1,256,2048]{2,1,0:T(8,128)(2,1)}, u32[]{:S(2)}) %copy-start) | copy-done | bytes 1048600
  1.9 0.0 copy-start.1
  1.9 1.2 %copy-done.1 = bf16[1,256,2048]{2,1,0:T(8,128)(2,1)S(1)} copy-done((bf16[1,256,2048]{2,1,0:T(8,128)(2,1)S(1)}, bf16[1,256,2048]{2,1,0:T(8,128)(2,1)}, u32[]{:S(2)}) %copy-start.1) | copy-done | bytes 1048600
  3.1 0.0 copy-start.2
  3.1 1.0 %copy-done.2 = bf16[1,256,1024]{2,1,0:T(8,128)(2,1)S(1)} copy-done((bf16[1,256,1024]{2,1,0:T(8,128)(2,1)S(1)}, bf16[1,256,1024]{2,1,0:T(8,128)(2,1)}, u32[]{:S(2)}) %copy-start.2) | copy-done | bytes 524312
  4.1 0.0 copy-start.3
  4.1 1.0 %copy-done.3 = bf16[1,256,1024]{2,1,0:T(8,128)(2,1)S(1)} copy-done((bf16[1,256,1024]{2,1,0:T(8,128)(2,1)S(1)}, bf16[1,256,1024]{2,1,0:T(8,128)(2,1)}, u32[]{:S(2)}) %copy-start.3) | copy-done | bytes 524312
  5.2 0.0 copy-start.4
  5.2 0.7 copy-done.4
  5.8 68.7 %shard_map.76 = (bf16[1,256,2048]{2,1,0:T(8,128)(2,1)S(1)}, bf16[1,256,1024]{2,1,0:T(8,128)(2,1)S(1)}, bf16[1,256,1024]{2,1,0:T(8,128)(2,1)S(1)}) custom-call(s32[4]{0:T(128)S(1)} %copy-done.4, bf16[1,256,2048]{2,1,0:T(8,128)(2,1)S(1)} %copy-done, bf16[1,256,1024]{2,1,0:T(8,128)(2,1)S(1)} %copy-done.2, bf16[1,256,1024]{2,1,0:T(8,128)(2,1)S(1)} %copy-done.3, ...), custom_call_target="tpu_custom_call" | custom-call | flops 6039797760 | bytes 8388608 | tf_op jit(solution)/shard_map/pallas_call | solution.py:327
  74.6 1.0 %copy.11 = bf16[1,256,2048]{2,1,0:T(8,128)(2,1)} copy(bf16[1,256,2048]{2,1,0:T(8,128)(2,1)S(1)} %get-tuple-element.6) | data formatting | bytes 2097152
  75.6 0.8 %copy.12 = bf16[1,256,1024]{2,1,0:T(8,128)(2,1)} copy(bf16[1,256,1024]{2,1,0:T(8,128)(2,1)S(1)} %get-tuple-element.7) | data formatting | bytes 1048576
  76.3 0.8 %copy.13 = bf16[1,256,1024]{2,1,0:T(8,128)(2,1)} copy(bf16[1,256,1024]{2,1,0:T(8,128)(2,1)S(1)} %get-tuple-element.8) | data formatting | bytes 1048576
Async XLA Ops:
  0.6 1.2 %copy-start = (bf16[1,256,2048]{2,1,0:T(8,128)(2,1)S(1)}, bf16[1,256,2048]{2,1,0:T(8,128)(2,1)}, u32[]{:S(2)}) copy-start(bf16[1,256,2048]{2,1,0:T(8,128)(2,1)} %q_in.1) | copy-start | bytes 3145732
  1.9 1.2 %copy-start.1 = (bf16[1,256,2048]{2,1,0:T(8,128)(2,1)S(1)}, bf16[1,256,2048]{2,1,0:T(8,128)(2,1)}, u32[]{:S(2)}) copy-start(bf16[1,256,2048]{2,1,0:T(8,128)(2,1)} %o_in.1) | copy-start | bytes 3145732
  3.1 1.0 %copy-start.2 = (bf16[1,256,1024]{2,1,0:T(8,128)(2,1)S(1)}, bf16[1,256,1024]{2,1,0:T(8,128)(2,1)}, u32[]{:S(2)}) copy-start(bf16[1,256,1024]{2,1,0:T(8,128)(2,1)} %k_in.1) | copy-start | bytes 1572868
  4.1 1.0 %copy-start.3 = (bf16[1,256,1024]{2,1,0:T(8,128)(2,1)S(1)}, bf16[1,256,1024]{2,1,0:T(8,128)(2,1)}, u32[]{:S(2)}) copy-start(bf16[1,256,1024]{2,1,0:T(8,128)(2,1)} %v_in.1) | copy-start | bytes 1572868
  5.2 0.7 copy-start.4

commit v2 on v1

--- a/solution.py
+++ b/solution.py
@@ -23,7 +23,7 @@
     docs, q_in, k_in, v_in, o_in,
     dq_out, dk_out, dv_out,
     q_buf, o_buf, kv_buf, kt_buf, bias_buf, acc_k, acc_v, term_buf, got_buf, dq_buf,
-    q_send, q_recv, o_send, o_recv, kv_send, kv_recv, g_send, g_recv, dq_send, dq_recv, dq_local,
+    q_send, q_recv, o_send, o_recv, kv_send, kv_recv, g_send, g_recv, dq_send, dq_recv, dq_local, relay_send, relay_recv,
 ):
     local_heads, chip_rows, group_width = q_buf.shape
     head_size = kt_buf.shape[0]
@@ -41,6 +41,16 @@
     sec_from = lax.rem(sec + 1, sections)
     sec_to = lax.rem(sec + sections - 1, sections)
 
+    relayed = chips == 4 and reach >= 2
+
+    def sends_to(away):
+        sends = chip + away < chips
+        return sends & (chip != 1) if relayed and away == 1 else sends
+
+    def gets_from(away):
+        gets = chip >= away
+        return gets & (chip != 2) if relayed and away == 1 else gets
+
     barrier = pltpu.get_barrier_semaphore()
 
     def greet(section, ctx):
@@ -124,6 +134,16 @@
             kv_recv.at[h, which, core],
         )
 
+    def copy_relay(h):
+        return pltpu.make_async_remote_copy(
+            src_ref=kv_buf.at[h, :, pl.ds((reach - 2) * chip_rows, chip_rows), :],
+            dst_ref=kv_buf.at[h, :, pl.ds((reach - 1) * chip_rows, chip_rows), :],
+            send_sem=relay_send.at[h],
+            recv_sem=relay_recv.at[h],
+            device_id=(sec, (chip - 1) * CORES + core),
+            device_id_type=MESH,
+        )
+
     def copy_term(h, away, t):
         return pltpu.make_async_remote_copy(
             src_ref=term_buf.at[h, :, kv_rows(away, t), :],
@@ -172,7 +192,7 @@
             copy_o(h, t, core).start()
         for which in range(2):
             for away in range(1, reach + 1):
-                @pl.when(chip + away < chips)
+                @pl.when(sends_to(away))
                 def _():
                     for t in range(CORES):
                         copy_kv(h, which, away, t, core).start()
@@ -214,6 +234,18 @@
 
     @pl.loop(0, local_heads)
     def _(h):
+        for away in range(reach, 0, -1):
+            @pl.when(gets_from(away))
+            def _():
+                for which in range(2):
+                    for c in range(CORES):
+                        copy_kv(h, which, away, c, c).wait_recv()
+
+            if relayed and away == 2:
+                @pl.when(chip == 3)
+                def _():
+                    copy_relay(h).start()
+
         copy_q_own(h).wait()
         copy_q_sibling(h, other).wait_recv()
         for which in range(2):
@@ -221,12 +253,10 @@
             copy_kv(h, which, 0, other, other).wait_recv()
         for c in range(CORES):
             copy_o(h, c, c).wait_recv()
-        for away in range(1, reach + 1):
-            @pl.when(chip >= away)
-            def _():
-                for which in range(2):
-                    for c in range(CORES):
-                        copy_kv(h, which, away, c, c).wait_recv()
+        if relayed:
+            @pl.when(chip == 2)
+            def _():
+                copy_relay(h).wait_recv()
 
         kt_buf[...] = kv_buf[h, 0].T
         acc_k[...] = jnp.zeros_like(acc_k)
@@ -297,8 +327,13 @@
         for which in range(2):
             copy_kv(h, which, 0, other, core).wait_send()
         copy_term(h, 0, other).wait_send()
+        if relayed:
+            @pl.when(chip == 3)
+            def _():
+                copy_relay(h).wait_send()
+
         for away in range(1, reach + 1):
-            @pl.when(chip + away < chips)
+            @pl.when(sends_to(away))
             def _():
                 for which in range(2):
                     for t in range(CORES):
@@ -355,9 +390,11 @@
             dma((local_heads,)),
             dma((local_heads,)),
             dma((local_heads,)),
+            dma((local_heads,)),
+            dma((local_heads,)),
         ],
         compiler_params=pltpu.CompilerParams(
-            collective_id=0, has_side_effects=True, vmem_limit_bytes=48 * 1024 * 1024
+            collective_id=0, has_side_effects=True, vmem_limit_bytes=63 * 1024 * 1024
         ),
         cost_estimate=pl.CostEstimate(
             flops=10 * pairs * head_size, bytes_accessed=8 * 1024 * 1024, transcendentals=pairs

time: 78.2 us -> 76.8 us (0.982)
  local copies, waits for them, and re-layouts: 7.74 us -> 4.39 us
  Pallas kernels: 68.7 us -> 70.7 us
    unnamed x13 -> x7, local copies, waits for them, and re-layouts: 7.74 us -> 4.39 us
    pallas_call x1, Pallas kernels: 68.7 us -> 70.7 us  [local(): pl.pallas_call(functools.partial(kernel, sections, chips), out_shape=(jax...]
where the time goes in v2:
time: 76.8 us; the launch traced here: 75.7 us
  Pallas kernels  70.7 us (92%)
  local copies, waits for them, and re-layouts  4.39 us (6%)
    pallas_call x1, Pallas kernels, local(): pl.pallas_call(functools.partial(kernel, sections, chips), out_shape=(jax...  70.7 us
    unnamed x7, local copies, waits for them, and re-layouts  4.39 us

profile of v2, /device:TPU:3, one launch (start us, length us, event | category | flops | bytes accessed | tf_op | source)
XLA Modules:
  0.0 75.7 jit_solution(2085761845433255186)
XLA Ops:
  0.6 70.7 %shard_map.76 = (bf16[1,256,2048]{2,1,0:T(8,128)(2,1)}, bf16[1,256,1024]{2,1,0:T(8,128)(2,1)}, bf16[1,256,1024]{2,1,0:T(8,128)(2,1)}) custom-call(s32[4]{0:T(128)} %docs.1, bf16[1,256,2048]{2,1,0:T(8,128)(2,1)} %q_in.1, bf16[1,256,1024]{2,1,0:T(8,128)(2,1)} %k_in.1, bf16[1,256,1024]{2,1,0:T(8,128)(2,1)} %v_in.1, bf16[1,256,2048]{2,1,0:T(8,128)(2,1)} %o_in.1), custom_call_target="tpu_custom_call" | custom-call | flops 6039797760 | bytes 8388608 | tf_op jit(solution)/shard_map/pallas_call | solution.py:362
  71.3 0.0 copy-start.1
  71.3 2.4 %copy.11 = bf16[1,256,2048]{2,1,0:T(8,128)(2,1)} copy(bf16[1,256,2048]{2,1,0:T(8,128)(2,1)} %get-tuple-element.6) | data formatting | bytes 2097152
  73.7 0.0 copy-done.1
  73.7 0.0 copy-start
  73.7 0.8 %copy.12 = bf16[1,256,1024]{2,1,0:T(8,128)(2,1)} copy(bf16[1,256,1024]{2,1,0:T(8,128)(2,1)S(1)} %copy-done.1) | data formatting | bytes 1048576
  74.5 0.4 copy-done
  74.9 0.8 %copy.13 = bf16[1,256,1024]{2,1,0:T(8,128)(2,1)} copy(bf16[1,256,1024]{2,1,0:T(8,128)(2,1)S(1)} %copy-done) | data formatting | bytes 1048576
Async XLA Ops:
  71.3 2.4 %copy-start.1 = (bf16[1,256,1024]{2,1,0:T(8,128)(2,1)S(1)}, bf16[1,256,1024]{2,1,0:T(8,128)(2,1)}, u32[]{:S(2)}) copy-start(bf16[1,256,1024]{2,1,0:T(8,128)(2,1)} %get-tuple-element.7) | copy-start | bytes 1572868
  73.7 1.2 %copy-start = (bf16[1,256,1024]{2,1,0:T(8,128)(2,1)S(1)}, bf16[1,256,1024]{2,1,0:T(8,128)(2,1)}, u32[]{:S(2)}) copy-start(bf16[1,256,1024]{2,1,0:T(8,128)(2,1)} %get-tuple-element.8) | copy-start | bytes 1572868

commit v3 on v2

--- a/solution.py
+++ b/solution.py
@@ -186,8 +186,7 @@
             dq_buf.at[h, rows_of(core), :], dq_out.at[0, :, group_cols(h, core)], dq_local.at[h]
         )
 
-    @pl.loop(0, local_heads)
-    def _(h):
+    def send_head(h):
         for t in range(CORES):
             copy_o(h, t, core).start()
         for which in range(2):
@@ -202,6 +201,8 @@
             copy_kv(h, which, 0, other, core).start()
             copy_kv_own(h, which).start()
 
+    send_head(0)
+
     for away in range(1, reach + 1):
         @pl.when(chip < away)
         def _():
@@ -257,6 +258,10 @@
             @pl.when(chip == 2)
             def _():
                 copy_relay(h).wait_recv()
+
+        @pl.when(h + 1 < local_heads)
+        def _():
+            send_head(h + 1)
 
         kt_buf[...] = kv_buf[h, 0].T
         acc_k[...] = jnp.zeros_like(acc_k)

time: 76.8 us -> 81.4 us (1.060)
  Pallas kernels: 70.7 us -> 75.9 us
    pallas_call x1, Pallas kernels: 70.7 us -> 75.9 us  [local(): pl.pallas_call(functools.partial(kernel, sections, chips), out_shape=(jax...]
where the time goes in v3:
time: 81.4 us; the launch traced here: 80.9 us
  Pallas kernels  75.9 us (93%)
  local copies, waits for them, and re-layouts  4.39 us (5%)
    pallas_call x1, Pallas kernels, local(): pl.pallas_call(functools.partial(kernel, sections, chips), out_shape=(jax...  75.9 us
    unnamed x7, local copies, waits for them, and re-layouts  4.39 us

profile of v3, /device:TPU:3, one launch (start us, length us, event | category | flops | bytes accessed | tf_op | source)
XLA Modules:
  0.0 80.9 jit_solution(7037667153736880464)
XLA Ops:
  0.6 75.9 %shard_map.76 = (bf16[1,256,2048]{2,1,0:T(8,128)(2,1)}, bf16[1,256,1024]{2,1,0:T(8,128)(2,1)}, bf16[1,256,1024]{2,1,0:T(8,128)(2,1)}) custom-call(s32[4]{0:T(128)} %docs.1, bf16[1,256,2048]{2,1,0:T(8,128)(2,1)} %q_in.1, bf16[1,256,1024]{2,1,0:T(8,128)(2,1)} %k_in.1, bf16[1,256,1024]{2,1,0:T(8,128)(2,1)} %v_in.1, bf16[1,256,2048]{2,1,0:T(8,128)(2,1)} %o_in.1), custom_call_target="tpu_custom_call" | custom-call | flops 6039797760 | bytes 8388608 | tf_op jit(solution)/shard_map/pallas_call | solution.py:367
  76.5 0.0 copy-start.1
  76.6 2.4 %copy.11 = bf16[1,256,2048]{2,1,0:T(8,128)(2,1)} copy(bf16[1,256,2048]{2,1,0:T(8,128)(2,1)} %get-tuple-element.6) | data formatting | bytes 2097152
  78.9 0.0 copy-done.1
  78.9 0.0 copy-start
  78.9 0.8 copy.12
  79.7 0.4 copy-done
  80.2 0.8 copy.13
Async XLA Ops:
  76.5 2.4 %copy-start.1 = (bf16[1,256,1024]{2,1,0:T(8,128)(2,1)S(1)}, bf16[1,256,1024]{2,1,0:T(8,128)(2,1)}, u32[]{:S(2)}) copy-start(bf16[1,256,1024]{2,1,0:T(8,128)(2,1)} %get-tuple-element.7) | copy-start | bytes 1572868
  78.9 1.2 %copy-start = (bf16[1,256,1024]{2,1,0:T(8,128)(2,1)S(1)}, bf16[1,256,1024]{2,1,0:T(8,128)(2,1)}, u32[]{:S(2)}) copy-start(bf16[1,256,1024]{2,1,0:T(8,128)(2,1)} %get-tuple-element.8) | copy-start | bytes 1572868

commit v4 on v2

--- a/solution.py
+++ b/solution.py
@@ -262,7 +262,7 @@
         acc_k[...] = jnp.zeros_like(acc_k)
         acc_v[...] = jnp.zeros_like(acc_v)
 
-        @pl.loop(0, tiles)
+        @pl.loop(0, tiles, unroll=2)
         def _(tile):
             span = pl.ds(pl.multiple_of(tile * TILE, TILE), width)
             here = aligned(tile * TILE, TILE)

time: 76.8 us -> 76.7 us (level)
  no operation moved by 1% of the time
where the time goes in v4:
time: 76.7 us; the launch traced here: 75.6 us
  Pallas kernels  70.6 us (92%)
  local copies, waits for them, and re-layouts  4.39 us (6%)
    pallas_call x1, Pallas kernels, local(): pl.pallas_call(functools.partial(kernel, sections, chips), out_shape=(jax...  70.6 us
    unnamed x7, local copies, waits for them, and re-layouts  4.39 us

profile of v4, /device:TPU:3, one launch (start us, length us, event | category | flops | bytes accessed | tf_op | source)
XLA Modules:
  0.0 75.6 jit_solution(12128740205599407765)
XLA Ops:
  0.6 70.6 %shard_map.76 = (bf16[1,256,2048]{2,1,0:T(8,128)(2,1)}, bf16[1,256,1024]{2,1,0:T(8,128)(2,1)}, bf16[1,256,1024]{2,1,0:T(8,128)(2,1)}) custom-call(s32[4]{0:T(128)} %docs.1, bf16[1,256,2048]{2,1,0:T(8,128)(2,1)} %q_in.1, bf16[1,256,1024]{2,1,0:T(8,128)(2,1)} %k_in.1, bf16[1,256,1024]{2,1,0:T(8,128)(2,1)} %v_in.1, bf16[1,256,2048]{2,1,0:T(8,128)(2,1)} %o_in.1), custom_call_target="tpu_custom_call" | custom-call | flops 6039797760 | bytes 8388608 | tf_op jit(solution)/shard_map/pallas_call | solution.py:362
  71.2 0.0 copy-start.1
  71.3 2.4 %copy.11 = bf16[1,256,2048]{2,1,0:T(8,128)(2,1)} copy(bf16[1,256,2048]{2,1,0:T(8,128)(2,1)} %get-tuple-element.6) | data formatting | bytes 2097152
  73.6 0.0 copy-done.1
  73.6 0.0 copy-start
  73.6 0.8 %copy.12 = bf16[1,256,1024]{2,1,0:T(8,128)(2,1)} copy(bf16[1,256,1024]{2,1,0:T(8,128)(2,1)S(1)} %copy-done.1) | data formatting | bytes 1048576
  74.4 0.4 copy-done
  74.8 0.8 %copy.13 = bf16[1,256,1024]{2,1,0:T(8,128)(2,1)} copy(bf16[1,256,1024]{2,1,0:T(8,128)(2,1)S(1)} %copy-done) | data formatting | bytes 1048576
Async XLA Ops:
  71.2 2.4 %copy-start.1 = (bf16[1,256,1024]{2,1,0:T(8,128)(2,1)S(1)}, bf16[1,256,1024]{2,1,0:T(8,128)(2,1)}, u32[]{:S(2)}) copy-start(bf16[1,256,1024]{2,1,0:T(8,128)(2,1)} %get-tuple-element.7) | copy-start | bytes 1572868
  73.6 1.2 %copy-start = (bf16[1,256,1024]{2,1,0:T(8,128)(2,1)S(1)}, bf16[1,256,1024]{2,1,0:T(8,128)(2,1)}, u32[]{:S(2)}) copy-start(bf16[1,256,1024]{2,1,0:T(8,128)(2,1)} %get-tuple-element.8) | copy-start | bytes 1572868

commit v5 on v4

--- a/solution.py
+++ b/solution.py
@@ -41,7 +41,7 @@
     sec_from = lax.rem(sec + 1, sections)
     sec_to = lax.rem(sec + sections - 1, sections)
 
-    relayed = chips == 4 and reach >= 2
+    relayed = False
 
     def sends_to(away):
         sends = chip + away < chips

time: 76.7 us -> 76.1 us (level)
  no operation moved by 1% of the time
where the time goes in v5:
time: 76.1 us; the launch traced here: 75 us
  Pallas kernels  70 us (92%)
  local copies, waits for them, and re-layouts  4.39 us (6%)
    pallas_call x1, Pallas kernels, local(): pl.pallas_call(functools.partial(kernel, sections, chips), out_shape=(jax...  70 us
    unnamed x7, local copies, waits for them, and re-layouts  4.39 us

profile of v5, /device:TPU:3, one launch (start us, length us, event | category | flops | bytes accessed | tf_op | source)
XLA Modules:
  0.0 75.0 jit_solution(17886639892767880299)
XLA Ops:
  0.6 70.0 %shard_map.76 = (bf16[1,256,2048]{2,1,0:T(8,128)(2,1)}, bf16[1,256,1024]{2,1,0:T(8,128)(2,1)}, bf16[1,256,1024]{2,1,0:T(8,128)(2,1)}) custom-call(s32[4]{0:T(128)} %docs.1, bf16[1,256,2048]{2,1,0:T(8,128)(2,1)} %q_in.1, bf16[1,256,1024]{2,1,0:T(8,128)(2,1)} %k_in.1, bf16[1,256,1024]{2,1,0:T(8,128)(2,1)} %v_in.1, bf16[1,256,2048]{2,1,0:T(8,128)(2,1)} %o_in.1), custom_call_target="tpu_custom_call" | custom-call | flops 6039797760 | bytes 8388608 | tf_op jit(solution)/shard_map/pallas_call | solution.py:362
  70.6 0.0 copy-start.1
  70.6 2.4 %copy.11 = bf16[1,256,2048]{2,1,0:T(8,128)(2,1)} copy(bf16[1,256,2048]{2,1,0:T(8,128)(2,1)} %get-tuple-element.6) | data formatting | bytes 2097152
  73.0 0.0 copy-done.1
  73.0 0.0 copy-start
  73.0 0.8 %copy.12 = bf16[1,256,1024]{2,1,0:T(8,128)(2,1)} copy(bf16[1,256,1024]{2,1,0:T(8,128)(2,1)S(1)} %copy-done.1) | data formatting | bytes 1048576
  73.8 0.4 copy-done
  74.2 0.8 %copy.13 = bf16[1,256,1024]{2,1,0:T(8,128)(2,1)} copy(bf16[1,256,1024]{2,1,0:T(8,128)(2,1)S(1)} %copy-done) | data formatting | bytes 1048576
Async XLA Ops:
  70.6 2.4 %copy-start.1 = (bf16[1,256,1024]{2,1,0:T(8,128)(2,1)S(1)}, bf16[1,256,1024]{2,1,0:T(8,128)(2,1)}, u32[]{:S(2)}) copy-start(bf16[1,256,1024]{2,1,0:T(8,128)(2,1)} %get-tuple-element.7) | copy-start | bytes 1572868
  73.0 1.2 %copy-start = (bf16[1,256,1024]{2,1,0:T(8,128)(2,1)S(1)}, bf16[1,256,1024]{2,1,0:T(8,128)(2,1)}, u32[]{:S(2)}) copy-start(bf16[1,256,1024]{2,1,0:T(8,128)(2,1)} %get-tuple-element.8) | copy-start | bytes 1572868
